TPU v7x, 32 devices: a whole 2x2x4 slice. The times are simulated.
32 devices in a mesh: replica: 4 (over z), shard: 4 (over y, core), tensor: 2 (over x).
Axes of the slice: x: 2, y: 2, z: 4, core: 2. Of those that a mesh axis runs over, the one named last changes fastest.
Arguments:
- trained_up: bfloat16 [4, 1024, 4096], P('replica', None, 'tensor'), may hold values from -6 to 6
- trained_down: bfloat16 [4, 4096, 1024], P('replica', 'tensor'), may hold values from -6 to 6
- trained_embed: bfloat16 [4, 8192, 1024], P('replica', ('shard', 'tensor')), may hold values from -6 to 6
- trained_norm: bfloat16 [4, 2, 1024], P('replica'), may hold values from 0.099609375 to 1.8984375
- master_up: float32 [1024, 4096], P(('replica', 'shard', 'tensor')), may hold values from -6 to 6
- moment_up: float32 [1024, 4096], P(('replica', 'shard', 'tensor')), may hold values from -4 to 4
- master_down: float32 [2, 2048, 1024], P('tensor', ('replica', 'shard')), may hold values from -6 to 6
- moment_down: float32 [2, 2048, 1024], P('tensor', ('replica', 'shard')), may hold values from -4 to 4
- master_embed: float32 [8, 1024, 1024], P(('shard', 'tensor'), 'replica'), may hold values from -6 to 6
- moment_embed: float32 [8, 1024, 64], P(('shard', 'tensor'), 'replica'), may hold values from -4 to 4
- master_norm: float32 [2, 1024], replicated, may hold values from 0.1 to 1.9
- moment_norm: float32 [2, 1024], replicated, may hold values from -2 to 2
- embed_basis: float32 [1024, 64], replicated, may hold values from -0.1875 to 0.1875
Outputs:
- recast_up: bfloat16 [1024, 4096], P(None, 'tensor')
- recast_down: bfloat16 [4096, 1024], P('tensor')
- recast_embed: bfloat16 [8192, 1024], P(('shard', 'tensor'))
- recast_norm: bfloat16 [2, 1024], replicated
- stored_up: float32 [1024, 4096], P(('replica', 'shard', 'tensor'))
- velocity_up: float32 [1024, 4096], P(('replica', 'shard', 'tensor'))
- stored_down: float32 [2, 2048, 1024], P('tensor', ('replica', 'shard'))
- velocity_down: float32 [2, 2048, 1024], P('tensor', ('replica', 'shard'))
- stored_embed: float32 [8, 1024, 1024], P(('shard', 'tensor'), 'replica')
- velocity_embed: float32 [8, 1024, 64], P(('shard', 'tensor'), 'replica')
- stored_norm: float32 [2, 1024], replicated
- velocity_norm: float32 [2, 1024], replicated
All inputs are finite; a program needn't handle non-finite values.
Results may differ from a plain program's by a relative error of at most 0.012.
Values may be sent and summed in bfloat16 or wider, within the bound.
No kernel may reach another device: no remote copies, remote signals or barrier semaphores. Data moves between devices by JAX's collectives and lax.ppermute only.
A program may use at most 128 MiB of HBM per device.

v0:
```python
import jax
import jax.numpy as jnp
from jax import lax
from jax.sharding import PartitionSpec as P


def outer_step(master, moment, summed, groups):
    difference = master - summed / groups
    velocity = 0.5 * moment + difference
    return (master - 0.7 * (difference + 0.5 * velocity), velocity)


def body(
    trained_up,
    trained_down,
    trained_embed,
    trained_norm,
    master_up,
    moment_up,
    master_down,
    moment_down,
    master_embed,
    moment_embed,
    master_norm,
    moment_norm,
    embed_basis,
):
    replicas = lax.axis_size("replica")
    shards = lax.axis_size("shard")
    tensors = lax.axis_size("tensor")
    shard_pos = lax.axis_index("shard")
    width = embed_basis.shape[0]
    rows_up = master_up.shape[0]
    half_cols = trained_up.shape[2]
    rows_down = master_down.shape[1]
    up_blocks = trained_up[0].reshape(replicas, shards, tensors, rows_up, half_cols)
    up_own = lax.dynamic_index_in_dim(up_blocks, shard_pos, 1, keepdims=False)
    down_blocks = trained_down[0].reshape(replicas, shards, rows_down, width)
    down_own = lax.dynamic_index_in_dim(down_blocks, shard_pos, 1, keepdims=False)
    up_summed, down_summed = (
        lax.psum_scatter(
            up_own.astype(jnp.float32).astype(jnp.bfloat16),
            "replica",
            scatter_dimension=0,
            tiled=True,
        ).astype(jnp.float32),
        lax.psum_scatter(
            down_own.astype(jnp.float32).astype(jnp.bfloat16),
            "replica",
            scatter_dimension=0,
            tiled=True,
        ).astype(jnp.float32),
    )
    up_summed = lax.all_to_all(up_summed, "tensor", split_axis=1, concat_axis=3, tiled=True)
    stored_up, velocity_up = outer_step(
        master_up, moment_up, up_summed.reshape(rows_up, half_cols * tensors), replicas
    )
    stored_down, velocity_down = outer_step(master_down, moment_down, down_summed, replicas)
    norm_summed = lax.psum(trained_norm[0].astype(jnp.float32), "replica")
    stored_norm, velocity_norm = outer_step(master_norm, moment_norm, norm_summed, replicas)
    embed_own = master_embed[0]
    rows_embed = embed_own.shape[0]
    embed_terms = trained_embed[0].reshape(replicas, rows_embed, width).astype(jnp.float32)
    embed_summed = lax.psum_scatter(
        embed_terms.astype(jnp.bfloat16), "replica", scatter_dimension=0, tiled=True
    ).astype(jnp.float32)[0]
    coefficient = jnp.dot(
        embed_own - embed_summed / replicas, embed_basis, precision=lax.Precision.HIGHEST
    )
    velocity_rows = 0.5 * moment_embed[0] + coefficient
    stored_rows = embed_own - 0.7 * jnp.dot(
        coefficient + 0.5 * velocity_rows, embed_basis.T, precision=lax.Precision.HIGHEST
    )
    up_piece = lax.all_to_all(
        stored_up.astype(jnp.bfloat16), "tensor", split_axis=1, concat_axis=0, tiled=True
    )
    down_piece = stored_down[0].astype(jnp.bfloat16)
    recast_up, recast_down = (
        lax.all_gather(up_piece, ("replica", "shard"), axis=0, tiled=True),
        lax.all_gather(down_piece, ("replica", "shard"), axis=0, tiled=True),
    )
    recast_embed = lax.all_gather(stored_rows.astype(jnp.bfloat16), "replica", axis=0, tiled=True)
    return (
        recast_up,
        recast_down,
        recast_embed,
        stored_norm.astype(jnp.bfloat16),
        stored_up,
        velocity_up,
        stored_down,
        velocity_down,
        stored_rows[None],
        velocity_rows[None],
        stored_norm,
        velocity_norm,
    )


def solution(mesh):
    in_specs = (
        P("replica", None, "tensor"),
        P("replica", "tensor", None),
        P("replica", ("shard", "tensor"), None),
        P("replica", None, None),
        P(("replica", "shard", "tensor"), None),
        P(("replica", "shard", "tensor"), None),
        P("tensor", ("replica", "shard"), None),
        P("tensor", ("replica", "shard"), None),
        P(("shard", "tensor"), "replica", None),
        P(("shard", "tensor"), "replica", None),
        P(),
        P(),
        P(),
    )
    out_specs = (
        P(None, "tensor"),
        P("tensor", None),
        P(("shard", "tensor"), None),
        P(),
        P(("replica", "shard", "tensor"), None),
        P(("replica", "shard", "tensor"), None),
        P("tensor", ("replica", "shard"), None),
        P("tensor", ("replica", "shard"), None),
        P(("shard", "tensor"), "replica", None),
        P(("shard", "tensor"), "replica", None),
        P(),
        P(),
    )
    return jax.shard_map(body, mesh=mesh, in_specs=in_specs, out_specs=out_specs, check_vma=False)
```

profile of v0, /device:TPU:0, one launch (start us, length us, event | category | flops | bytes accessed | tf_op | source)
XLA Modules:
  0.0 281.9 jit_solution(11830214835437392084)
XLA Ops:
  7.2 0.7 reduce-scatter.8.cloned.1.call-update
  8.0 2.3 dynamic-slice_bitcast_fusion
  10.4 2.4 dynamic-slice_bitcast_fusion.1
  12.8 44.1 %reduce-scatter.8.cloned.1.call-done = bf16[1,256,1024]{2,1,0:T(8,128)(2,1)} async-done(((bf16[4,256,1024]{2,1,0:T(8,128)(2,1)}), bf16[1,256,1024]{2,1,0:T(8,128)(2,1)}) %reduce-scatter.8.cloned.1.call-update) | async-done | bytes 524304 | tf_op jit(solution)/shard_map/reduce_scatter | solution.py:64
  56.9 2.2 fusion.1
  59.1 2.2 fusion.16
  61.4 25.0 %reduce-scatter.6.cloned.1.call-done = bf16[1,128,1024]{2,1,0:T(8,128)(2,1)} async-done(((bf16[4,128,1024]{2,1,0:T(8,128)(2,1)}), bf16[1,128,1024]{2,1,0:T(8,128)(2,1)}) %reduce-scatter.6.cloned.1.call-update) | async-done | bytes 262160 | tf_op jit(solution)/shard_map/reduce_scatter | solution.py:47
  86.4 2.2 fusion.14
  88.6 26.5 %reduce-scatter.4.cloned.1.call-done = bf16[1,2,32,2048]{3,2,1,0:T(8,128)(2,1)} async-done(((bf16[4,2,32,2048]{3,2,1,0:T(8,128)(2,1)}), bf16[1,2,32,2048]{3,2,1,0:T(8,128)(2,1)}) %reduce-scatter.4.cloned.1.call-update) | async-done | bytes 262160 | tf_op jit(solution)/shard_map/reduce_scatter | solution.py:41
  115.1 1.0 bitcast_convert_fusion
  116.1 10.6 %all_to_all.28 = f32[1,2,32,2048]{3,2,0,1:T(8,128)S(1)} all-to-all(f32[1,2,32,2048]{3,2,0,1:T(8,128)S(1)} %bitcast_convert_fusion), channel_id=1, replica_groups=mesh['replica'=4,'shard'=4,'tensor'=2] {'tensor'}, dimensions={1} | all-to-all | bytes 1048576 | tf_op jit(solution)/shard_map/all_to_all | solution.py:54
  126.8 0.4 copy.33
  127.5 1.1 fusion.15
  128.6 8.3 %all_to_all.29 = bf16[32,2,2048]{2,0,1:T(8,128)(2,1)} all-to-all(bf16[32,2,2048]{2,0,1:T(8,128)(2,1)S(1)} %bitcast.61), channel_id=1, replica_groups=mesh['replica'=4,'shard'=4,'tensor'=2] {'tensor'}, dimensions={1} | all-to-all | bytes 524288 | tf_op jit(solution)/shard_map/all_to_all | solution.py:74
  137.0 10.4 %psum.7 = f32[2,1024]{1,0:T(2,128)S(1)} all-reduce(f32[2,1024]{1,0:T(2,128)S(1)} %bitcast_convert_fusion.1), channel_id=1, replica_groups=mesh['replica'=4,'shard'=4,'tensor'=2] {'replica'}, use_global_device_ids=true, to_apply=%region_3.4 | all-reduce | flops 2048 | bytes 16384 | tf_op jit(solution)/shard_map/psum | solution.py:59
  147.4 0.6 fusion.13
  148.0 0.6 fusion.8
  148.6 13.6 %all-gather.7.cloned.1.call-done = bf16[1024,1024]{1,0:T(8,128)(2,1)} async-done(((bf16[256,1024]{1,0:T(8,128)(2,1)}), bf16[1024,1024]{1,0:T(8,128)(2,1)}) %all-gather.7.cloned.1.call-update) | async-done | bytes 2097168 | tf_op jit(solution)/shard_map/all_gather | solution.py:82
  162.2 52.2 %all-gather.9.cloned.1.call-done = bf16[1,2048,1024]{2,1,0:T(8,128)(2,1)} async-done(((bf16[1,128,1024]{2,1,0:T(8,128)(2,1)}), bf16[1,2048,1024]{2,1,0:T(8,128)(2,1)}) %all-gather.9.cloned.1.call-update) | async-done | bytes 4194320 | tf_op jit(solution)/shard_map/all_gather | solution.py:80
  214.4 51.3 %all-gather.5.cloned.1.call-done = bf16[1024,2048]{1,0:T(8,128)(2,1)} async-done(((bf16[64,2048]{1,0:T(8,128)(2,1)}), bf16[1024,2048]{1,0:T(8,128)(2,1)}) %all-gather.5.cloned.1.call-update) | async-done | bytes 4194320 | tf_op jit(solution)/shard_map/all_gather | solution.py:79
  265.7 4.9 %copy.45 = bf16[1024,2048]{1,0:T(8,128)(2,1)} copy(bf16[1024,2048]{1,0:T(8,128)(2,1)} %all-gather.5.cloned.1.call-done) | data formatting | bytes 8388608
  270.7 2.1 copy.46
  272.8 1.0 copy-done.3
  273.8 1.3 copy.47
  (38 shorter events, 0.8 us)
Async XLA Ops:
  7.2 49.7 %copy-start = (f32[1024,64]{0,1:T(8,128)S(1)}, f32[1024,64]{0,1:T(8,128)}, u32[]{:S(2)}) copy-start(f32[1024,64]{0,1:T(8,128)} %param.25) | copy-start | bytes 786436
  7.2 49.7 %reduce-scatter.8.cloned.1.call-start = ((), (), s32[]{:S(2)}) async-start(), calls=%async_computation.8 | async-start | bytes 2621440 | tf_op jit(solution)/shard_map/reduce_scatter | solution.py:64
  7.2 49.7 %copy-start.1 = (f32[1,256,1024]{2,1,0:T(8,128)S(1)}, f32[1,256,1024]{2,1,0:T(8,128)}, u32[]{:S(2)}) copy-start(f32[1,256,1024]{2,1,0:T(8,128)} %param.21) | copy-start | bytes 3145732
  7.9 51.2 %copy-start.8 = (f32[1,256,64]{1,2,0:T(8,128)S(1)}, f32[1,256,64]{1,2,0:T(8,128)}, u32[]{:S(2)}) copy-start(f32[1,256,64]{1,2,0:T(8,128)} %param.22) | copy-start | bytes 196612
  7.9 78.4 %reduce-scatter.6.cloned.1.call-start = ((), (), s32[]{:S(2)}) async-start(), calls=%async_computation.7 | async-start | bytes 1310720 | tf_op jit(solution)/shard_map/reduce_scatter | solution.py:47
  10.3 104.8 %reduce-scatter.4.cloned.1.call-start = ((), (), s32[]{:S(2)}) async-start(), calls=%async_computation.5 | async-start | bytes 1310720 | tf_op jit(solution)/shard_map/reduce_scatter | solution.py:41
  10.3 76.0 %copy-start.4 = (f32[1,128,1024]{2,1,0:T(8,128)S(1)}, f32[1,128,1024]{2,1,0:T(8,128)}, u32[]{:S(2)}) copy-start(f32[1,128,1024]{2,1,0:T(8,128)} %param.19) | copy-start | bytes 1572868
  10.3 76.0 %copy-start.5 = (f32[1,128,1024]{2,1,0:T(8,128)S(1)}, f32[1,128,1024]{2,1,0:T(8,128)}, u32[]{:S(2)}) copy-start(f32[1,128,1024]{2,1,0:T(8,128)} %param.20) | copy-start | bytes 1572868
  12.8 149.4 %all-gather.7.cloned.1.call-start = ((), (), s32[]{:S(2)}) async-start(), calls=%async_computation.9 | async-start | bytes 2621440 | tf_op jit(solution)/shard_map/all_gather | solution.py:82
  61.3 66.2 %copy-start.6 = (f32[32,4096]{1,0:T(8,128)S(1)}, f32[32,4096]{1,0:T(8,128)}, u32[]{:S(2)}) copy-start(f32[32,4096]{1,0:T(8,128)} %param.17) | copy-start | bytes 1572868
  61.3 66.2 %copy-start.7 = (f32[32,4096]{1,0:T(8,128)S(1)}, f32[32,4096]{1,0:T(8,128)}, u32[]{:S(2)}) copy-start(f32[32,4096]{1,0:T(8,128)} %param.18) | copy-start | bytes 1572868
  61.3 153.1 %all-gather.9.cloned.1.call-start = ((), (), s32[]{:S(2)}) async-start(), calls=%async_computation.10 | async-start | bytes 4456448 | tf_op jit(solution)/shard_map/all_gather | solution.py:80
  88.5 177.2 %all-gather.5.cloned.1.call-start = ((), (), s32[]{:S(2)}) async-start(), calls=%async_computation.6 | async-start | bytes 4456448 | tf_op jit(solution)/shard_map/all_gather | solution.py:79
  116.1 20.9 %copy-start.11 = (bf16[1,2,1024]{2,1,0:T(2,128)(2,1)S(1)}, bf16[1,2,1024]{2,1,0:T(2,128)(2,1)}, u32[]{:S(2)}) copy-start(bf16[1,2,1024]{2,1,0:T(2,128)(2,1)} %param.16) | copy-start | bytes 12292
  116.1 31.3 %copy-start.9 = (f32[2,1024]{1,0:T(2,128)S(1)}, f32[2,1024]{1,0:T(2,128)}, u32[]{:S(2)}) copy-start(f32[2,1024]{1,0:T(2,128)} %param.23) | copy-start | bytes 24580
  116.1 31.3 %copy-start.10 = (f32[2,1024]{1,0:T(2,128)S(1)}, f32[2,1024]{1,0:T(2,128)}, u32[]{:S(2)}) copy-start(f32[2,1024]{1,0:T(2,128)} %param.24) | copy-start | bytes 24580
  265.7 4.9 %copy-start.2 = (bf16[1,2048,1024]{2,1,0:T(8,128)(2,1)S(1)}, bf16[1,2048,1024]{2,1,0:T(8,128)(2,1)}, u32[]{:S(2)}) copy-start(bf16[1,2048,1024]{2,1,0:T(8,128)(2,1)} %all-gather.9.cloned.1.call-done) | copy-start | bytes 12582916
  270.7 3.1 %copy-start.3 = (bf16[1024,1024]{1,0:T(8,128)(2,1)S(1)}, bf16[1024,1024]{1,0:T(8,128)(2,1)}, u32[]{:S(2)}) copy-start(bf16[1024,1024]{1,0:T(8,128)(2,1)} %all-gather.7.cloned.1.call-done) | copy-start | bytes 6291460
Sparse Core Ops, SparseCore 0:
  10.3 46.5 reduce-scatter.7
  59.9 26.4 reduce-scatter.5
  89.2 25.7 reduce-scatter.3
  117.1 45.0 all-gather.6
  165.0 49.3 all-gather.8
  216.7 49.0 all-gather.4
where the time goes:
time: 282 us
  waiting for transfers between devices  213 us (76%)
  blocking collectives  29.3 us (10%)
  local copies, waits for them, and re-layouts  14.8 us (5%)
  between operations  14.3 us (5%)
  other arithmetic  5.54 us (2%)
  matrix products  4.38 us (2%)
    all_gather x1, waiting for transfers between devices, body(): lax.all_gather(down_piece, ('replica', 'shard'), axis=0, tiled=True)  52.2 us
    all_gather x1, waiting for transfers between devices, body(): lax.all_gather(up_piece, ('replica', 'shard'), axis=0, tiled=True)  51.3 us
    reduce_scatter x1, waiting for transfers between devices, body(): lax.psum_scatter(embed_terms.astype(jnp.bfloat16), 'replica', scatter_dim...  44.1 us
    reduce_scatter x1, waiting for transfers between devices, body(): lax.psum_scatter(up_own.astype(jnp.float32).astype(jnp.bfloat16), 'replic...  26.5 us
    reduce_scatter x1, waiting for transfers between devices, body(): lax.psum_scatter(down_own.astype(jnp.float32).astype(jnp.bfloat16), 'repl...  25 us
    all_gather x1, waiting for transfers between devices, body(): lax.all_gather(stored_rows.astype(jnp.bfloat16), 'replica', axis=0, tiled...  13.6 us
    all_to_all x1, blocking collectives, body(): lax.all_to_all(up_summed, 'tensor', split_axis=1, concat_axis=3, tiled=True)  10.6 us
    psum x1, blocking collectives, body(): norm_summed = lax.psum(trained_norm[0].astype(jnp.float32), 'replica')  10.4 us
  transfers between devices with their start and end apart: 6, of which 6 were waited for; matrix products, arithmetic and copies ran while one was open for 5% of the time, Pallas kernels for 0%

commit v1 on v0

v1 whole, which is shorter than its diff:
```python
import functools

import jax
import jax.numpy as jnp
from jax import lax
from jax.experimental import pallas as pl
from jax.experimental.pallas import tpu as pltpu
from jax.sharding import PartitionSpec as P

F32 = jnp.float32
BF16 = jnp.bfloat16


def outer_step(master, moment, summed, groups):
    difference = master - summed / groups
    velocity = 0.5 * moment + difference
    return (master - 0.7 * (difference + 0.5 * velocity), velocity)


def line_reduce(block, replicas, pos):
    right = left = None
    for step in range(1, replicas):
        ahead = block(jnp.minimum(pos + replicas - step, replicas - 1))
        behind = block(jnp.maximum(pos - replicas + step, 0))
        if right is not None:
            ahead = (ahead.astype(F32) + right.astype(F32)).astype(BF16)
            behind = (behind.astype(F32) + left.astype(F32)).astype(BF16)
        right = lax.ppermute(ahead, "replica", [(i, i + 1) for i in range(step)])
        left = lax.ppermute(
            behind, "replica", [(i, i - 1) for i in range(replicas - step, replicas)]
        )
    return block(pos).astype(F32) + right.astype(F32) + left.astype(F32)


def gather_pieces(piece, replicas, shards, pos):
    top = shards // 2

    def across(x, valid):
        pairs = [(i * shards + j, i * shards + (j ^ top)) for i in valid for j in range(shards)]
        return lax.ppermute(x, ("replica", "shard"), pairs)

    rights, lefts, far_rights, far_lefts = [None], [None], [None], [None]
    right = left = piece
    far = across(piece, range(replicas))
    for step in range(1, replicas):
        right = lax.ppermute(right, "replica", [(i, i + 1) for i in range(step - 1, replicas - 1)])
        left = lax.ppermute(left, "replica", [(i, i - 1) for i in range(1, replicas - step + 1)])
        rights.append(right)
        lefts.append(left)
        far_rights.append(across(right, range(step, replicas)))
        far_lefts.append(across(left, range(replicas - step)))
    pairs = {(0, 0): jnp.stack([piece, far])}
    for slot in range(1, replicas):
        below = pos >= slot
        pairs[slot, 0] = jnp.stack(
            [
                jnp.where(below, rights[slot], lefts[replicas - slot]),
                jnp.where(below, far_rights[slot], far_lefts[replicas - slot]),
            ]
        )
    bit = top // 2
    while bit:
        for (slot, mask), pair in list(pairs.items()):
            swapped = lax.ppermute(pair, "shard", [(j, j ^ bit) for j in range(shards)])
            pairs[slot, mask ^ bit] = swapped
        bit //= 2
    return pairs


def place_kernel(keys, replicas, top, *refs):
    sources, out, sem = refs[: len(keys)], refs[len(keys)], refs[len(keys) + 1]
    pos, me = lax.axis_index("replica"), lax.axis_index("shard")
    copies = []
    for source, (slot, mask) in zip(sources, keys):
        owner = lax.rem(pos + replicas - slot, replicas)
        for half in range(2):
            shard = jnp.bitwise_xor(me, mask ^ (top * half))
            copy = pltpu.make_async_copy(
                source.at[half], out.at[owner, shard], sem.at[len(copies)]
            )
            copy.start()
            copies.append(copy)
    for copy in copies:
        copy.wait()


def place(pairs, replicas, shards):
    keys = list(pairs)
    sources = [pairs[key] for key in keys]
    piece = sources[0].shape[1:]
    size = 2 * len(keys) * sources[0].size
    return pl.pallas_call(
        functools.partial(place_kernel, keys, replicas, shards // 2),
        out_shape=jax.ShapeDtypeStruct((replicas, shards) + piece, BF16),
        in_specs=[pl.BlockSpec(memory_space=pl.ANY)] * len(keys),
        out_specs=pl.BlockSpec(memory_space=pl.ANY),
        scratch_shapes=[pltpu.SemaphoreType.DMA((2 * len(keys),))],
        cost_estimate=pl.CostEstimate(flops=0, bytes_accessed=2 * size, transcendentals=0),
        name="place_pieces",
    )(*sources)


def body(
    trained_up,
    trained_down,
    trained_embed,
    trained_norm,
    master_up,
    moment_up,
    master_down,
    moment_down,
    master_embed,
    moment_embed,
    master_norm,
    moment_norm,
    embed_basis,
):
    replicas = lax.axis_size("replica")
    shards = lax.axis_size("shard")
    tensors = lax.axis_size("tensor")
    pos = lax.axis_index("replica")
    shard_pos = lax.axis_index("shard")
    tensor_pos = lax.axis_index("tensor")
    width, rank = embed_basis.shape
    rows_up = master_up.shape[0]
    half_cols = trained_up.shape[2]
    rows_down = master_down.shape[1]
    rows_embed = master_embed.shape[1]

    high = lax.reduce_precision(embed_basis, 8, 7)
    middle = lax.reduce_precision(embed_basis - high, 8, 7)
    low = embed_basis - high - middle
    split = jnp.concatenate([high, middle, low], axis=1).astype(BF16)
    projected = lax.dot_general(
        split, trained_embed[0], (((0,), (1,)), ((), ())), preferred_element_type=F32
    )
    projected = projected[:rank] + projected[rank : 2 * rank] + projected[2 * rank :]
    norm_own = trained_norm[0].astype(F32).reshape(-1, rows_embed)

    def packet(owner):
        block = lax.dynamic_slice_in_dim(projected, owner * rows_embed, rows_embed, axis=1)
        return jnp.concatenate([block, norm_own], axis=0)

    packets = packet(pos)
    for shift in range(1, replicas):
        packets = packets + lax.ppermute(
            packet(lax.rem(pos + shift, replicas)),
            "replica",
            [(i, (i + shift) % replicas) for i in range(replicas)],
        )
    norm_summed = packets[rank:].reshape(master_norm.shape)
    stored_norm, velocity_norm = outer_step(master_norm, moment_norm, norm_summed, replicas)
    embed_own = master_embed[0]
    coefficient = (
        lax.dot_general(
            embed_basis, embed_own, (((0,), (1,)), ((), ())), precision=lax.Precision.HIGHEST
        )
        - packets[:rank] / replicas
    )
    velocity_rows = 0.5 * moment_embed[0].T + coefficient
    stored_rows = embed_own - 0.7 * lax.dot_general(
        coefficient + 0.5 * velocity_rows,
        embed_basis,
        (((0,), (1,)), ((), ())),
        precision=lax.Precision.HIGHEST,
    )
    recast_embed = lax.all_gather(stored_rows.astype(BF16), "replica", axis=0, tiled=True)

    down_blocks = trained_down[0].reshape(replicas, shards, rows_down, width)

    def down_block(owner):
        return lax.dynamic_slice(
            down_blocks, (owner, shard_pos, 0, 0), (1, 1, rows_down, width)
        ).reshape(rows_down, width)

    down_summed = line_reduce(down_block, replicas, pos)
    stored_down, velocity_down = outer_step(master_down, moment_down, down_summed[None], replicas)
    recast_down = place(
        gather_pieces(stored_down[0].astype(BF16), replicas, shards, pos), replicas, shards
    ).reshape(-1, width)

    up_blocks = trained_up[0].reshape(replicas, shards, tensors, rows_up, half_cols)

    def up_rows(tensor):
        return lax.dynamic_slice(
            up_blocks,
            (0, shard_pos, tensor, 0, 0),
            (replicas, 1, 1, rows_up, half_cols),
        ).reshape(replicas, 1, rows_up, half_cols)

    halves = jnp.arange(tensors).reshape(1, tensors, 1, 1)
    up_whole = up_rows(tensor_pos)
    for shift in range(1, tensors):
        came = lax.ppermute(
            up_rows(lax.rem(tensor_pos + shift, tensors)),
            "tensor",
            [(i, (i + shift) % tensors) for i in range(tensors)],
        )
        source = lax.rem(tensor_pos + tensors - shift, tensors)
        up_whole = jnp.where(halves == source, came, up_whole)

    def up_block(owner):
        return lax.dynamic_index_in_dim(up_whole, owner, 0, keepdims=False)

    up_summed = line_reduce(up_block, replicas, pos)
    up_summed = jnp.concatenate([up_summed[i] for i in range(tensors)], axis=1)
    stored_up, velocity_up = outer_step(master_up, moment_up, up_summed, replicas)
    up_recast = stored_up.astype(BF16)

    def up_cols(tensor):
        return lax.dynamic_slice_in_dim(up_recast, tensor * half_cols, half_cols, axis=1)[None]

    up_piece = up_cols(tensor_pos)
    for shift in range(1, tensors):
        came = lax.ppermute(
            up_cols(lax.rem(tensor_pos + shift, tensors)),
            "tensor",
            [(i, (i + shift) % tensors) for i in range(tensors)],
        )
        source = lax.rem(tensor_pos + tensors - shift, tensors)
        up_piece = jnp.where(halves[0] == source, came, up_piece)
    up_piece = up_piece.reshape(tensors * rows_up, half_cols)
    recast_up = place(
        gather_pieces(up_piece, replicas, shards, pos), replicas, shards
    ).reshape(-1, half_cols)

    return (
        recast_up,
        recast_down,
        recast_embed,
        stored_norm.astype(BF16),
        stored_up,
        velocity_up,
        stored_down,
        velocity_down,
        stored_rows[None],
        velocity_rows.T[None],
        stored_norm,
        velocity_norm,
    )


def solution(mesh):
    in_specs = (
        P("replica", None, "tensor"),
        P("replica", "tensor", None),
        P("replica", ("shard", "tensor"), None),
        P("replica", None, None),
        P(("replica", "shard", "tensor"), None),
        P(("replica", "shard", "tensor"), None),
        P("tensor", ("replica", "shard"), None),
        P("tensor", ("replica", "shard"), None),
        P(("shard", "tensor"), "replica", None),
        P(("shard", "tensor"), "replica", None),
        P(),
        P(),
        P(),
    )
    out_specs = (
        P(None, "tensor"),
        P("tensor", None),
        P(("shard", "tensor"), None),
        P(),
        P(("replica", "shard", "tensor"), None),
        P(("replica", "shard", "tensor"), None),
        P("tensor", ("replica", "shard"), None),
        P("tensor", ("replica", "shard"), None),
        P(("shard", "tensor"), "replica", None),
        P(("shard", "tensor"), "replica", None),
        P(),
        P(),
    )
    return jax.shard_map(body, mesh=mesh, in_specs=in_specs, out_specs=out_specs, check_vma=False)
```

time: 282 us -> 463 us (1.64)
  Pallas kernels: 0 us -> 257 us
  waiting for transfers between devices: 213 us -> 62.4 us
  starting transfers between devices: 0.24 us -> 83.6 us
  blocking collectives: 29.3 us -> 0 us
  other arithmetic: 5.54 us -> 25.1 us
    pallas_call x0 -> x2, Pallas kernels: none -> 257 us  [place(): pl.pallas_call(functools.partial(place_kernel, keys, replicas, shards //...]
    all_gather x3 -> x1, waiting for transfers between devices: 117 us -> 0.02 us  [body(): lax.all_gather(stored_rows.astype(BF16), 'replica', axis=0, tiled=True)]
    reduce_scatter x3 -> x0, waiting for transfers between devices: 95.5 us -> none  [the longest x1 44.1 us: body(): lax.psum_scatter(embed_terms.astype(jnp.bfloat16), 'replica', scatter_dim...]
    ppermute x0 -> x51, starting transfers between devices: none -> 83.6 us  [the longest x6 26.8 us: line_reduce(): right = lax.ppermute(ahead, 'replica', [(i, i + 1) for i in range(step)])]
    ppermute x0 -> x51, waiting for transfers between devices: none -> 62.4 us  [the longest x6 45 us: gather_pieces(): lax.ppermute(left, 'replica', [(i, i - 1) for i in range(1, replicas - st...]
    all_to_all x2 -> x0, blocking collectives: 18.9 us -> none  [the longest x1 10.6 us: body(): lax.all_to_all(up_summed, 'tensor', split_axis=1, concat_axis=3, tiled=True)]
    psum x1 -> x0, blocking collectives: 10.4 us -> none  [body(): norm_summed = lax.psum(trained_norm[0].astype(jnp.float32), 'replica')]
    convert_element_type x5 -> x9, other arithmetic: 4.86 us -> 12.2 us  [the longest x4 5.18 us: line_reduce(): ahead = (ahead.astype(F32) + right.astype(F32)).astype(BF16)]
  transfers between devices with their start and end apart: 6 -> 52, of which waited for: 6 -> 10; matrix products, arithmetic and copies ran while one was open for 5% -> 8% of each run, Pallas kernels for 0% -> 28%
where the time goes in v1:
time: 463 us; the launch traced here: 462 us
  Pallas kernels  257 us (56%)
  starting transfers between devices  83.6 us (18%)
  waiting for transfers between devices  62.4 us (13%)
  other arithmetic  25.1 us (5%)
  between operations  15 us (3%)
  local copies, waits for them, and re-layouts  13.5 us (3%)
  matrix products  5.36 us (1%)
    pallas_call x2, Pallas kernels, place(): pl.pallas_call(functools.partial(place_kernel, keys, replicas, shards //...  257 us
    ppermute x6, waiting for transfers between devices, gather_pieces(): lax.ppermute(left, 'replica', [(i, i - 1) for i in range(1, replicas - st...  45 us
    ppermute x6, starting transfers between devices, line_reduce(): right = lax.ppermute(ahead, 'replica', [(i, i + 1) for i in range(step)])  26.8 us
    ppermute x14, starting transfers between devices, across(): return lax.ppermute(x, ('replica', 'shard'), pairs)  25.3 us
    ppermute x6, starting transfers between devices, gather_pieces(): lax.ppermute(right, 'replica', [(i, i + 1) for i in range(step - 1, repli...  12.5 us
    ppermute x14, waiting for transfers between devices, across(): return lax.ppermute(x, ('replica', 'shard'), pairs)  11.3 us
  transfers between devices with their start and end apart: 52, of which 10 were waited for; matrix products, arithmetic and copies ran while one was open for 8% of the time, Pallas kernels for 28%

profile of v1, /device:TPU:0, one launch (start us, length us, event | category | flops | bytes accessed | tf_op | source)
XLA Modules:
  0.0 461.7 jit_solution(10585735670323513801)
XLA Ops:
  9.2 5.6 %collective-permute-start.25 = (bf16[128,1024]{1,0:T(8,128)(2,1)S(1)}, bf16[128,1024]{1,0:T(8,128)(2,1)}, u32[]{:S(2)}, u32[]{:S(2)}) collective-permute-start(bf16[128,1024]{1,0:T(8,128)(2,1)S(1)} %get-tuple-element.23), channel_id=1, source_target_pairs={{0,8},{1,9},{2,10},{3,11},{4,12},{5,13},{6,14},{7,15}} | collective-permute-start | bytes 786440 | tf_op jit(solution)/shard_map/ppermute | solution.py:28
  27.2 5.6 %collective-permute-start.26 = (bf16[128,1024]{1,0:T(8,128)(2,1)}, bf16[128,1024]{1,0:T(8,128)(2,1)}, u32[]{:S(2)}, u32[]{:S(2)}) collective-permute-start(bf16[128,1024]{1,0:T(8,128)(2,1)} %fusion.8), channel_id=1, source_target_pairs={{0,8},{8,16},{1,9},{9,17},{2,10},{10,18},{3,11},{11,19},{4,12},{12... | collective-permute-start | bytes 786440 | tf_op jit(solution)/shard_map/ppermute | solution.py:28
  46.7 4.4 collective-permute-start.2
  52.1 5.2 %collective-permute-start.27 = (bf16[128,1024]{1,0:T(8,128)(2,1)S(1)}, bf16[128,1024]{1,0:T(8,128)(2,1)S(1)}, u32[]{:S(2)}, u32[]{:S(2)}) collective-permute-start(bf16[128,1024]{1,0:T(8,128)(2,1)S(1)} %get-tuple-element.21), channel_id=1, source_target_pairs={{0,8},{8,16},{16,24},{1,9},{9,17},{17,25},{2,10},{10,18},{18,26},{... | collective-permute-start | bytes 786440 | tf_op jit(solution)/shard_map/ppermute | solution.py:28
  61.2 5.4 %collective-permute-done.30 = bf16[128,1024]{1,0:T(8,128)(2,1)S(1)} collective-permute-done((bf16[128,1024]{1,0:T(8,128)(2,1)S(1)}, bf16[128,1024]{1,0:T(8,128)(2,1)S(1)}, u32[]{:S(2)}, u32[]{:S(2)}) %collective-permute-start.30) | collective-permute-done | bytes 262176 | tf_op jit(solution)/shard_map/ppermute | solution.py:29
  70.1 5.2 %collective-permute-start.32 = (bf16[128,1024]{1,0:T(8,128)(2,1)}, bf16[128,1024]{1,0:T(8,128)(2,1)}, u32[]{:S(2)}, u32[]{:S(2)}) collective-permute-start(bf16[128,1024]{1,0:T(8,128)(2,1)} %bitcast.36), channel_id=1, source_target_pairs={{0,8},{8,16},{16,24},{1,9},{9,17},{17,25},{2,10},{10,18},{18,26},{... | collective-permute-start | bytes 786440 | tf_op jit(solution)/shard_map/ppermute | solution.py:46
  76.9 4.0 collective-permute-start.3
  85.2 2.4 collective-permute-start.43
  96.2 3.0 collective-permute-done.34
  99.2 3.7 collective-permute-start.40
  105.3 30.1 %collective-permute-done.35 = bf16[128,1024]{1,0:T(8,128)(2,1)S(1)} collective-permute-done((bf16[128,1024]{1,0:T(8,128)(2,1)S(1)}, bf16[128,1024]{1,0:T(8,128)(2,1)S(1)}, u32[]{:S(2)}, u32[]{:S(2)}) %collective-permute-start.35) | collective-permute-done | bytes 262176 | tf_op jit(solution)/shard_map/ppermute | solution.py:47
  139.8 4.6 collective-permute-start.9
  144.8 2.9 collective-permute-start.37
  149.9 3.2 collective-permute-done.37
  154.8 4.4 collective-permute-done.11
  159.2 2.9 collective-permute-start.17
  163.4 7.5 %collective-permute-done.12 = bf16[64,2048]{1,0:T(8,128)(2,1)S(1)} collective-permute-done((bf16[64,2048]{1,0:T(8,128)(2,1)S(1)}, bf16[64,2048]{1,0:T(8,128)(2,1)S(1)}, u32[]{:S(2)}, u32[]{:S(2)}) %collective-permute-start.12) | collective-permute-done | bytes 262176 | tf_op jit(solution)/shard_map/ppermute | solution.py:47
  172.4 3.5 collective-permute-start.20
  177.4 3.2 collective-permute-done.20
  181.4 3.6 collective-permute-start.14
  185.2 4.5 collective-permute-done.14
  194.3 128.3 %place_pieces.3 = bf16[4,4,128,1024]{3,2,1,0:T(8,128)(2,1)} custom-call(bf16[2,128,1024]{2,1,0:T(8,128)(2,1)} %copy-done.3, bf16[2,128,1024]{2,1,0:T(8,128)(2,1)} %copy-done.6, bf16[2,128,1024]{2,1,0:T(8,128)(2,1)} %copy-done.5, bf16[2,128,1024]{2,1,0:T(8,128)(2,1)} %pad_maximum_fusion.7.refs_3_, bf16[2,128,1024]{2,1,0:T(8,128)(2,1)} %copy-done.8, ...), custom_call_target="tpu_custom_call" | custom-call | bytes 8388608 | tf_op jit(solution)/shard_map/place_pieces/pallas_call | solution.py:92
  323.4 128.3 %place_pieces.2 = bf16[4,4,64,2048]{3,2,1,0:T(8,128)(2,1)} custom-call(bf16[2,64,2048]{2,1,0:T(8,128)(2,1)} %copy-done.4, bf16[2,64,2048]{2,1,0:T(8,128)(2,1)} %pad_maximum_fusion.1.refs_1_, bf16[2,64,2048]{2,1,0:T(8,128)(2,1)} %pad_maximum_fusion.2.refs_2_, bf16[2,64,2048]{2,1,0:T(8,128)(2,1)} %pad_maximum_fusion.3.refs_3_, bf16[2,64,2048]{2,1,0:T(8,128)(2,1)} %copy-done.7, ...), custom_call_target="tpu_custom_call" | custom-call | bytes 8388608 | tf_op jit(solution)/shard_map/place_pieces/pallas_call | solution.py:92
  451.7 3.1 copy.26
  (183 shorter events, 72.0 us)
Async XLA Ops:
  7.2 315.4 %all-gather.2.cloned.1.call-start = ((), (), s32[]{:S(2)}) async-start(), calls=%async_computation | async-start | bytes 2621440 | tf_op jit(solution)/shard_map/all_gather | solution.py:167
  9.2 16.3 %collective-permute-start.25 = (bf16[128,1024]{1,0:T(8,128)(2,1)S(1)}, bf16[128,1024]{1,0:T(8,128)(2,1)}, u32[]{:S(2)}, u32[]{:S(2)}) collective-permute-start(bf16[128,1024]{1,0:T(8,128)(2,1)S(1)} %get-tuple-element.23), channel_id=1, source_target_pairs={{0,8},{1,9},{2,10},{3,11},{4,12},{5,13},{6,14},{7,15}} | collective-permute-start | bytes 786440 | tf_op jit(solution)/shard_map/ppermute | solution.py:28
  17.1 15.8 %collective-permute-start = (bf16[4,1,32,2048]{3,2,0,1:T(8,128)(2,1)}, bf16[4,1,32,2048]{3,2,0,1:T(8,128)(2,1)S(1)}, u32[]{:S(2)}, u32[]{:S(2)}) collective-permute-start(bf16[4,1,32,2048]{3,2,0,1:T(8,128)(2,1)} %get-tuple-element.25), channel_id=1, source_target_pairs={{0,1},{1,0},{2,3},{3,2},{4,5},{5,4},{6,7},{7,6},{8,9},{9,8},{10,11... | collective-permute-start | bytes 1572872 | tf_op jit(solution)/shard_map/ppermute | solution.py:194
  22.7 24.0 %collective-permute-start.48 = (f32[72,256]{1,0:T(8,128)}, f32[72,256]{1,0:T(8,128)S(1)}, u32[]{:S(2)}, u32[]{:S(2)}) collective-permute-start(f32[72,256]{1,0:T(8,128)} %get-tuple-element.42), channel_id=1, source_target_pairs={{0,8},{8,16},{16,24},{24,0},{1,9},{9,17},{17,25},{25,1},{2,10},{10... | collective-permute-start | bytes 221192 | tf_op jit(solution)/shard_map/ppermute | solution.py:146
  22.7 28.4 %collective-permute-start.49 = (f32[72,256]{1,0:T(8,128)}, f32[72,256]{1,0:T(8,128)}, u32[]{:S(2)}, u32[]{:S(2)}) collective-permute-start(f32[72,256]{1,0:T(8,128)} %get-tuple-element.43), channel_id=1, source_target_pairs={{0,16},{8,24},{16,0},{24,8},{1,17},{9,25},{17,1},{25,9},{2,18},{10... | collective-permute-start | bytes 221192 | tf_op jit(solution)/shard_map/ppermute | solution.py:146
  24.1 18.6 %collective-permute-start.28 = (bf16[128,1024]{1,0:T(8,128)(2,1)}, bf16[128,1024]{1,0:T(8,128)(2,1)}, u32[]{:S(2)}, u32[]{:S(2)}) collective-permute-start(bf16[128,1024]{1,0:T(8,128)(2,1)} %get-tuple-element.24), channel_id=1, source_target_pairs={{24,16},{25,17},{26,18},{27,19},{28,20},{29,21},{30,22},{31,23}} | collective-permute-start | bytes 786440 | tf_op jit(solution)/shard_map/ppermute | solution.py:29
  27.2 15.5 %collective-permute-start.26 = (bf16[128,1024]{1,0:T(8,128)(2,1)}, bf16[128,1024]{1,0:T(8,128)(2,1)}, u32[]{:S(2)}, u32[]{:S(2)}) collective-permute-start(bf16[128,1024]{1,0:T(8,128)(2,1)} %fusion.8), channel_id=1, source_target_pairs={{0,8},{8,16},{1,9},{9,17},{2,10},{10,18},{3,11},{11,19},{4,12},{12... | collective-permute-start | bytes 786440 | tf_op jit(solution)/shard_map/ppermute | solution.py:28
  45.0 14.6 %collective-permute-start.4 = (bf16[2,32,2048]{2,1,0:T(8,128)(2,1)}, bf16[2,32,2048]{2,1,0:T(8,128)(2,1)S(1)}, u32[]{:S(2)}, u32[]{:S(2)}) collective-permute-start(bf16[2,32,2048]{2,1,0:T(8,128)(2,1)} %get-tuple-element.30), channel_id=1, source_target_pairs={{24,16},{25,17},{26,18},{27,19},{28,20},{29,21},{30,22},{31,23}} | collective-permute-start | bytes 786440 | tf_op jit(solution)/shard_map/ppermute | solution.py:29
  60.5 20.4 %collective-permute-start.5 = (bf16[2,32,2048]{2,1,0:T(8,128)(2,1)S(1)}, bf16[2,32,2048]{2,1,0:T(8,128)(2,1)S(1)}, u32[]{:S(2)}, u32[]{:S(2)}) collective-permute-start(bf16[2,32,2048]{2,1,0:T(8,128)(2,1)S(1)} %get-tuple-element.28), channel_id=1, source_target_pairs={{16,8},{24,16},{17,9},{25,17},{18,10},{26,18},{19,11},{27,19},{20,... | collective-permute-start | bytes 786440 | tf_op jit(solution)/shard_map/ppermute | solution.py:29
  68.8 16.3 %collective-permute-start.33 = (bf16[128,1024]{1,0:T(8,128)(2,1)}, bf16[128,1024]{1,0:T(8,128)(2,1)}, u32[]{:S(2)}, u32[]{:S(2)}) collective-permute-start(bf16[128,1024]{1,0:T(8,128)(2,1)} %bitcast.36), channel_id=1, source_target_pairs={{8,0},{16,8},{24,16},{9,1},{17,9},{25,17},{10,2},{18,10},{26,18},{... | collective-permute-start | bytes 786440 | tf_op jit(solution)/shard_map/ppermute | solution.py:47
  70.1 17.5 %collective-permute-start.32 = (bf16[128,1024]{1,0:T(8,128)(2,1)}, bf16[128,1024]{1,0:T(8,128)(2,1)}, u32[]{:S(2)}, u32[]{:S(2)}) collective-permute-start(bf16[128,1024]{1,0:T(8,128)(2,1)} %bitcast.36), channel_id=1, source_target_pairs={{0,8},{8,16},{16,24},{1,9},{9,17},{17,25},{2,10},{10,18},{18,26},{... | collective-permute-start | bytes 786440 | tf_op jit(solution)/shard_map/ppermute | solution.py:46
  76.9 13.8 %collective-permute-start.3 = (bf16[2,32,2048]{2,1,0:T(8,128)(2,1)}, bf16[2,32,2048]{2,1,0:T(8,128)(2,1)}, u32[]{:S(2)}, u32[]{:S(2)}) collective-permute-start(bf16[2,32,2048]{2,1,0:T(8,128)(2,1)} %get-tuple-element.27), channel_id=1, source_target_pairs={{0,8},{8,16},{16,24},{1,9},{9,17},{17,25},{2,10},{10,18},{18,26},{... | collective-permute-start | bytes 786440 | tf_op jit(solution)/shard_map/ppermute | solution.py:28
  85.2 54.6 %collective-permute-start.43 = (bf16[128,1024]{1,0:T(8,128)(2,1)}, bf16[128,1024]{1,0:T(8,128)(2,1)S(1)}, u32[]{:S(2)}, u32[]{:S(2)}) collective-permute-start(bf16[128,1024]{1,0:T(8,128)(2,1)} %collective-permute-done.33), channel_id=1, source_target_pairs={{0,4},{2,6},{4,0},{6,2},{8,12},{10,14},{12,8},{14,10},{16,20},{18,... | collective-permute-start | bytes 786440 | tf_op jit(solution)/shard_map/ppermute | solution.py:40
  88.9 14.0 %collective-permute-start.38 = (bf16[128,1024]{1,0:T(8,128)(2,1)}, bf16[128,1024]{1,0:T(8,128)(2,1)S(1)}, u32[]{:S(2)}, u32[]{:S(2)}) collective-permute-start(bf16[128,1024]{1,0:T(8,128)(2,1)} %collective-permute-done.32), channel_id=1, source_target_pairs={{8,16},{16,24},{9,17},{17,25},{10,18},{18,26},{11,19},{19,27},{12,... | collective-permute-start | bytes 786440 | tf_op jit(solution)/shard_map/ppermute | solution.py:46
  90.7 57.2 %collective-permute-start.36 = (bf16[128,1024]{1,0:T(8,128)(2,1)}, bf16[128,1024]{1,0:T(8,128)(2,1)S(1)}, u32[]{:S(2)}, u32[]{:S(2)}) collective-permute-start(bf16[128,1024]{1,0:T(8,128)(2,1)} %collective-permute-done.32), channel_id=1, source_target_pairs={{8,12},{10,14},{12,8},{14,10},{16,20},{18,22},{20,16},{22,18},{24,... | collective-permute-start | bytes 786440 | tf_op jit(solution)/shard_map/ppermute | solution.py:40
  99.2 39.1 %collective-permute-start.40 = (bf16[128,1024]{1,0:T(8,128)(2,1)S(1)}, bf16[128,1024]{1,0:T(8,128)(2,1)S(1)}, u32[]{:S(2)}, u32[]{:S(2)}) collective-permute-start(bf16[128,1024]{1,0:T(8,128)(2,1)S(1)} %collective-permute-done.34), channel_id=1, source_target_pairs={{0,4},{2,6},{4,0},{6,2},{8,12},{10,14},{12,8},{14,10},{1,5},{3,7},... | collective-permute-start | bytes 786440 | tf_op jit(solution)/shard_map/ppermute | solution.py:40
  103.0 32.4 %collective-permute-start.35 = (bf16[128,1024]{1,0:T(8,128)(2,1)S(1)}, bf16[128,1024]{1,0:T(8,128)(2,1)S(1)}, u32[]{:S(2)}, u32[]{:S(2)}) collective-permute-start(bf16[128,1024]{1,0:T(8,128)(2,1)S(1)} %collective-permute-done.34), channel_id=1, source_target_pairs={{8,0},{9,1},{10,2},{11,3},{12,4},{13,5},{14,6},{15,7}} | collective-permute-start | bytes 786440 | tf_op jit(solution)/shard_map/ppermute | solution.py:47
  104.3 31.7 %collective-permute-start.41 = (bf16[128,1024]{1,0:T(8,128)(2,1)S(1)}, bf16[128,1024]{1,0:T(8,128)(2,1)S(1)}, u32[]{:S(2)}, u32[]{:S(2)}) collective-permute-start(bf16[128,1024]{1,0:T(8,128)(2,1)S(1)} %collective-permute-done.38), channel_id=1, source_target_pairs={{16,24},{17,25},{18,26},{19,27},{20,28},{21,29},{22,30},{23,31}} | collective-permute-start | bytes 786440 | tf_op jit(solution)/shard_map/ppermute | solution.py:46
  147.9 43.5 %collective-permute-start.44 = (bf16[2,128,1024]{2,1,0:T(8,128)(2,1)S(1)}, bf16[2,128,1024]{2,1,0:T(8,128)(2,1)S(1)}, u32[]{:S(2)}, u32[]{:S(2)}) collective-permute-start(bf16[2,128,1024]{2,1,0:T(8,128)(2,1)S(1)} %pad_maximum_fusion.4.refs_0_), channel_id=1, source_target_pairs={{0,2},{2,0},{4,6},{6,4},{1,3},{3,1},{5,7},{7,5},{8,10},{10,8},{12,... | collective-permute-start | bytes 1572872 | tf_op jit(solution)/shard_map/ppermute | solution.py:64
  148.0 43.9 %collective-permute-start.46 = (bf16[2,128,1024]{2,1,0:T(8,128)(2,1)S(1)}, bf16[2,128,1024]{2,1,0:T(8,128)(2,1)S(1)}, u32[]{:S(2)}, u32[]{:S(2)}) collective-permute-start(bf16[2,128,1024]{2,1,0:T(8,128)(2,1)S(1)} %pad_maximum_fusion.6.refs_2_), channel_id=1, source_target_pairs={{0,2},{2,0},{4,6},{6,4},{1,3},{3,1},{5,7},{7,5},{8,10},{10,8},{12,... | collective-permute-start | bytes 1572872 | tf_op jit(solution)/shard_map/ppermute | solution.py:64
  148.6 174.1 %collective-permute-start.21 = (bf16[2,64,2048]{2,1,0:T(8,128)(2,1)S(1)}, bf16[2,64,2048]{2,1,0:T(8,128)(2,1)S(1)}, u32[]{:S(2)}, u32[]{:S(2)}) collective-permute-start(bf16[2,64,2048]{2,1,0:T(8,128)(2,1)S(1)} %pad_maximum_fusion.refs_0_), channel_id=1, source_target_pairs={{0,2},{2,0},{4,6},{6,4},{1,3},{3,1},{5,7},{7,5},{8,10},{10,8},{12,... | collective-permute-start | bytes 1572872 | tf_op jit(solution)/shard_map/ppermute | solution.py:64
  191.4 131.3 %collective-permute-start.23 = (bf16[2,64,2048]{2,1,0:T(8,128)(2,1)}, bf16[2,64,2048]{2,1,0:T(8,128)(2,1)}, u32[]{:S(2)}, u32[]{:S(2)}) collective-permute-start(bf16[2,64,2048]{2,1,0:T(8,128)(2,1)} %pad_maximum_fusion.2.refs_2_), channel_id=1, source_target_pairs={{0,2},{2,0},{4,6},{6,4},{1,3},{3,1},{5,7},{7,5},{8,10},{10,8},{12,... | collective-permute-start | bytes 1572872 | tf_op jit(solution)/shard_map/ppermute | solution.py:64
  191.9 130.8 %collective-permute-start.22 = (bf16[2,64,2048]{2,1,0:T(8,128)(2,1)}, bf16[2,64,2048]{2,1,0:T(8,128)(2,1)}, u32[]{:S(2)}, u32[]{:S(2)}) collective-permute-start(bf16[2,64,2048]{2,1,0:T(8,128)(2,1)} %pad_maximum_fusion.1.refs_1_), channel_id=1, source_target_pairs={{0,2},{2,0},{4,6},{6,4},{1,3},{3,1},{5,7},{7,5},{8,10},{10,8},{12,... | collective-permute-start | bytes 1572872 | tf_op jit(solution)/shard_map/ppermute | solution.py:64
  192.2 130.5 %collective-permute-start.24 = (bf16[2,64,2048]{2,1,0:T(8,128)(2,1)}, bf16[2,64,2048]{2,1,0:T(8,128)(2,1)}, u32[]{:S(2)}, u32[]{:S(2)}) collective-permute-start(bf16[2,64,2048]{2,1,0:T(8,128)(2,1)} %pad_maximum_fusion.3.refs_3_), channel_id=1, source_target_pairs={{0,2},{2,0},{4,6},{6,4},{1,3},{3,1},{5,7},{7,5},{8,10},{10,8},{12,... | collective-permute-start | bytes 1572872 | tf_op jit(solution)/shard_map/ppermute | solution.py:64
  (50 other events, 729.8 us)
Sparse Core Ops, SparseCore 0:
  85.3 53.9 all-gather.1
